TPU v7x, 512 devices: a whole 4x8x8 slice. The times are simulated.
512 devices in a mesh: exp: 64 (over x, y, core), rep: 8 (over z).
Axes of the slice: x: 4, y: 8, z: 8, core: 2. Of those that a mesh axis runs over, the one named last changes fastest.
Arguments:
- passages_in: bfloat16 [92160, 2048], P(('exp', 'rep')), may hold values from -24 to 32
- routes: int32 [92160, 2], P(('exp', 'rep')), may hold values from 0 to 63, all different within a row; in each aligned block of 180 rows (0 to 179, 180 to 359, ...) at most 11 rows name the same one
- route_weights: float32 [92160, 2], P(('exp', 'rep')), may hold values from 0.2 to 1
- gate_weight: bfloat16 [64, 2048, 704], P('exp', 'rep'), may hold values from -0.125 to 0.125
- up_weight: bfloat16 [64, 2048, 704], P('exp', 'rep'), may hold values from -0.125 to 0.125
- down_weight: bfloat16 [64, 704, 2048], P('exp', None, 'rep'), may hold values from -0.21875 to 0.21875
- projection: bfloat16 [2048, 128], replicated, may hold values from -2 to 2
- queries: bfloat16 [128, 32, 128], P('rep'), may hold values from -6 to 6
- positives: int32 [128], replicated, may hold values from 0 to 511, as said below
Outputs:
- states: bfloat16 [92160, 2048], P(('exp', 'rep'))
- grad_projection: float32 [2048, 128], P('exp')
- mean_loss: float32 [], replicated
Inputs may be any that keep to these rules, and one draw needn't show every extreme that they name: `routes`: the two experts of a token differ. Among the rows of one device, no expert is named more than 11 times, and in some device's rows some expert is named exactly 11 times; every expert is named somewhere. `positives`: distinct queries have distinct positive passages.
All inputs are finite; a program needn't handle non-finite values.
Results may differ from a plain program's by a relative error of at most 0.0065.
Values may be sent and summed in bfloat16 or wider, within the bound.
No kernel may reach another device: no remote copies, remote signals or barrier semaphores. Data moves between devices by JAX's collectives and lax.ppermute only.
A program may use at most 64 MiB of HBM per device.

v0:
```python
import jax
import jax.numpy as jnp
from jax import lax
from jax.sharding import PartitionSpec as P

PAS_LEN = 180
soft_temp = 0.05
logit_gain = 1.5
norm_eps = 1e-06


def unit_rows(values):
    values = values.astype(jnp.float32)
    radius = jnp.sqrt(jnp.sum(values * values, axis=-1, keepdims=True) + norm_eps)
    return (values / radius, radius)


def token_scores(unit_block, query_rows, passage_count, query_count):
    scores = lax.dot_general(
        unit_block, query_rows, (((1,), (1,)), ((), ())), preferred_element_type=jnp.float32
    )
    weights = jnp.exp(scores / soft_temp)
    passage_len = unit_block.shape[0] // passage_count
    totals = jnp.sum(weights.reshape(passage_count, passage_len, -1), axis=1)
    logits = logit_gain * jnp.sum(
        (soft_temp * jnp.log(totals)).reshape(passage_count, query_count, -1), axis=2
    )
    return (weights, totals, logits)


def unit_grads(weights, totals, factor, query_rows, passage_count, query_count):
    passage_len = weights.shape[0] // passage_count
    query_len = weights.shape[1] // query_count
    shaped = weights.reshape(passage_count, passage_len, query_count, query_len) / totals.reshape(
        passage_count, 1, query_count, query_len
    )
    coeffs = (shaped * (logit_gain * factor)[:, None, :, None]).astype(jnp.bfloat16)
    coeffs = coeffs.reshape(passage_count * passage_len, query_count * query_len)
    return jnp.dot(coeffs, query_rows, preferred_element_type=jnp.float32)


def body(
    passages_in,
    routes,
    route_weights,
    gate_weight,
    up_weight,
    down_weight,
    projection,
    queries,
    positives,
):
    tok_count, model_width = passages_in.shape
    top_count = routes.shape[1]
    experts = lax.axis_size("exp")
    rep_count = lax.axis_size("rep")
    capacity = max(2, 2 * tok_count * top_count // experts)
    flat_route = routes.reshape(-1)
    onehot = (flat_route[:, None] == jnp.arange(experts, dtype=jnp.int32)[None, :]).astype(
        jnp.int32
    )
    slot_rank = jnp.sum((jnp.cumsum(onehot, axis=0) - onehot) * onehot, axis=1)
    places = flat_route * capacity + slot_rank
    sources = jnp.arange(tok_count * top_count, dtype=jnp.int32) // top_count
    outgoing = (
        jnp.zeros((experts * capacity, model_width), jnp.bfloat16)
        .at[places]
        .set(passages_in[sources])
    )
    arrived = lax.all_to_all(
        outgoing.reshape(experts, capacity, model_width),
        "exp",
        split_axis=0,
        concat_axis=0,
        tiled=True,
    )
    expert_rows = arrived.reshape(experts * capacity, model_width)

    def add_rows(shard_part):
        return jnp.dot(expert_rows, shard_part[0], preferred_element_type=jnp.float32)

    gate_sum = add_rows(lax.all_gather(gate_weight, "rep", axis=1, tiled=True))
    up_sum = add_rows(lax.all_gather(up_weight, "rep", axis=1, tiled=True))
    hidden = (jax.nn.silu(gate_sum) * up_sum).astype(jnp.bfloat16)
    expert_out = jnp.dot(
        hidden,
        lax.all_gather(down_weight, "rep", axis=2, tiled=True)[0],
        preferred_element_type=jnp.float32,
    ).astype(jnp.bfloat16)
    returned = lax.all_to_all(
        expert_out.reshape(experts, capacity, model_width),
        "exp",
        split_axis=0,
        concat_axis=0,
        tiled=True,
    )
    picked = returned.reshape(experts * capacity, model_width)[places].reshape(
        tok_count, top_count, model_width
    )
    mixed_sum = passages_in.astype(jnp.float32) + jnp.sum(
        route_weights[:, :, None] * picked.astype(jnp.float32), axis=1
    )
    states = mixed_sum.astype(jnp.bfloat16)
    projected = jnp.dot(states, projection, preferred_element_type=jnp.float32)
    unit_f32, radius = unit_rows(projected)
    unit_vec = unit_f32.astype(jnp.bfloat16)
    query_unit = unit_rows(queries)[0].astype(jnp.bfloat16)
    query_block, query_len, unit_width = queries.shape
    pas_count = tok_count // PAS_LEN
    total_queries = query_block * rep_count
    all_queries = lax.all_gather(query_unit, "rep", axis=0, tiled=True)
    query_rows = all_queries.reshape(total_queries * query_len, unit_width)
    owners = lax.axis_index(("exp", "rep")) * pas_count + jnp.arange(pas_count, dtype=jnp.int32)
    weights, totals, logits = token_scores(unit_vec, query_rows, pas_count, total_queries)
    positive_hit = owners[:, None] == positives[None, :]
    exp_logits = jnp.exp(logits)
    partition, pos_sum = lax.psum(
        (jnp.sum(exp_logits, axis=0), jnp.sum(jnp.where(positive_hit, logits, 0.0))), ("exp", "rep")
    )
    mean_loss = (jnp.sum(jnp.log(partition)) - pos_sum) / total_queries
    factor = exp_logits / partition[None, :] - positive_hit.astype(jnp.float32)
    grad_unit = unit_grads(weights, totals, factor, query_rows, pas_count, total_queries)
    grad_vec = (
        (grad_unit - unit_f32 * jnp.sum(unit_f32 * grad_unit, axis=1, keepdims=True)) / radius
    ).astype(jnp.bfloat16)
    row_sums = lax.psum_scatter(
        lax.dot_general(
            states, grad_vec, (((0,), (0,)), ((), ())), preferred_element_type=jnp.float32
        ),
        "exp",
        scatter_dimension=0,
        tiled=True,
    )
    grad_projection = lax.psum(row_sums, "rep")
    return (states, grad_projection, mean_loss)


def solution(mesh):
    in_specs = (
        P(("exp", "rep"), None),
        P(("exp", "rep"), None),
        P(("exp", "rep"), None),
        P("exp", "rep", None),
        P("exp", "rep", None),
        P("exp", None, "rep"),
        P(),
        P("rep", None, None),
        P(),
    )
    out_specs = (P(("exp", "rep"), None), P("exp", None), P())
    return jax.shard_map(body, mesh=mesh, in_specs=in_specs, out_specs=out_specs, check_vma=False)
```

profile of v0, /device:TPU:16, one launch (start us, length us, event | category | flops | bytes accessed | tf_op | source)
XLA Modules:
  0.0 605.3 jit_solution(8828364484753994428)
XLA Ops:
  7.2 0.0 copy-start
  7.2 0.0 all-gather.5.cloned.1.call-start
  7.2 0.7 all-gather.5.cloned.1.call-update
  7.9 0.0 all-gather.7.cloned.1.call-start
  8.0 0.7 all-gather.7.cloned.1.call-update
  8.7 0.8 copy.20
  9.5 0.1 eq.31
  9.7 0.9 reduce-window.6
  10.6 0.2 slice_reduce_fusion
  10.8 0.7 broadcast_multiply_fusion
  11.5 0.1 copy.19
  11.6 0.1 mul.100
  11.8 0.1 bitcast_bitcast_fusion
  12.0 8.1 %scatter_custom_fusion = bf16[704,2048]{1,0:T(8,128)(2,1)S(1)} fusion(s32[360]{0:T(512)S(1)} %fusion.22, bf16[180,2048]{1,0:T(8,128)(2,1)} %param.9, s32[1024]{0:T(1024)S(1)} %pad_clamp_fusion.1, bf16[]{:T(256)} %constant.21.clone.1), kind=kCustom, calls=%fused_computation.16 | custom fusion | bytes 2884096 | tf_op jit(solution)/shard_map/scatter | solution.py:68
  20.1 2.9 reshape.185
  23.0 10.8 %all-to-all-start = ((bf16[64,11,2048]{2,1,0:T(8,128)(2,1)}), bf16[64,11,2048]{2,1,0:T(8,128)(2,1)}, u32[]{:S(2)}, u32[]{:S(2)}) async-start(bf16[64,11,2048]{2,1,0:T(8,128)(2,1)} %reshape.185), calls=%async_computation | async-start | bytes 8388608 | tf_op jit(solution)/shard_map/all_to_all | solution.py:70
  33.7 0.2 all-gather.9.cloned.1.call-start
  34.0 0.5 all-gather.9.cloned.1.call-update
  34.5 93.6 %all-to-all-done = bf16[64,11,2048]{2,1,0:T(8,128)(2,1)} async-done(((bf16[64,11,2048]{2,1,0:T(8,128)(2,1)}), bf16[64,11,2048]{2,1,0:T(8,128)(2,1)}, u32[]{:S(2)}, u32[]{:S(2)}) %all-to-all-start) | async-done | bytes 2883616 | tf_op jit(solution)/shard_map/all_to_all | solution.py:70
  128.1 3.4 reshape.186
  131.5 0.0 all-gather.5.cloned.1.call-done
  131.5 5.6 fusion.4
  137.1 44.8 %all-gather.9.cloned.1.call-done = bf16[1,704,2048]{2,1,0:T(8,128)(2,1)} async-done(((bf16[1,704,256]{2,1,0:T(8,128)(2,1)}), bf16[1,704,2048]{2,1,0:T(8,128)(2,1)}) %all-gather.9.cloned.1.call-update) | async-done | bytes 2883600 | tf_op jit(solution)/shard_map/all_gather | solution.py:87
  181.9 10.4 %convolution_convert_fusion = bf16[704,2048]{1,0:T(8,128)(2,1)} fusion(bf16[1,704,2048]{2,1,0:T(8,128)(2,1)} %all-gather.9.cloned.1.call-done, f32[704,704]{1,0:T(8,128)} %fusion.4, bf16[704,2048]{1,0:T(8,128)(2,1)S(1)} %reshape.186, bf16[1,2048,704]{1,2,0:T(8,128)(2,1)} %all-gather.7.cloned.1.call-done), kind=kOutput, calls=%fused_computation.5 | convolution fusion | flops 4064501760 | bytes 13516800 | tf_op jit(solution)/shard_map/dot_general | solution.py:85
  192.3 4.8 reshape.187
  197.1 10.5 %all-to-all-start.1 = ((bf16[64,11,2048]{2,1,0:T(8,128)(2,1)}), bf16[64,11,2048]{2,1,0:T(8,128)(2,1)}, u32[]{:S(2)}, u32[]{:S(2)}) async-start(bf16[64,11,2048]{2,1,0:T(8,128)(2,1)} %reshape.187), calls=%async_computation.1 | async-start | bytes 8388608 | tf_op jit(solution)/shard_map/all_to_all | solution.py:90
  207.6 0.0 all-gather.11.cloned.1.call-start
  207.7 0.0 copy-done.4
  207.7 0.1 fusion.14
  207.8 0.8 fusion.15
  208.6 0.0 all-gather.11.cloned.1.call-update
  208.7 0.3 reduce-scatter.2.cloned.1.call-start
  208.9 0.0 copy-done.5
  209.0 0.8 copy.18
  209.7 92.1 %all-to-all-done.1 = bf16[64,11,2048]{2,1,0:T(8,128)(2,1)} async-done(((bf16[64,11,2048]{2,1,0:T(8,128)(2,1)}), bf16[64,11,2048]{2,1,0:T(8,128)(2,1)}, u32[]{:S(2)}, u32[]{:S(2)}) %all-to-all-start.1) | async-done | bytes 2883616 | tf_op jit(solution)/shard_map/all_to_all | solution.py:90
  301.9 3.4 reshape.188
  305.3 3.1 gather_fusion
  308.4 3.4 reshape.191
  311.7 0.0 copy-start.3
  311.8 5.6 multiply_reduce_fusion
  317.3 0.0 copy-done.3
  317.3 0.2 add_convert_fusion
  317.5 0.0 copy-done
  317.5 0.0 copy-start.1
  317.5 0.0 copy-start.6
  317.5 0.5 multiply_reduce_fusion.2
  318.0 0.0 all-gather.11.cloned.1.call-done
  318.0 0.0 copy-start.2
  318.0 3.8 fusion.28
  321.9 0.1 mul.109
  321.9 0.1 reduce_sum.93
  322.0 0.0 copy-done.6
  322.1 0.6 fusion.26
  322.7 96.3 %all-reduce.1 = (f32[128]{0:T(128)S(1)}, f32[]{:T(128)}) all-reduce(f32[128]{0:T(128)S(1)} %get-tuple-element.8, f32[]{:T(128)} %get-tuple-element.7), channel_id=1, replica_groups=mesh['exp'=64,'rep'=8] {'exp','rep'}, use_global_device_ids=true, to_apply=%region_9.10 | all-reduce | flops 129 | bytes 1032 | tf_op jit(solution)/shard_map/psum | solution.py:117
  418.9 0.6 log_reduce_fusion
  419.5 0.1 mul.113
  419.6 0.1 mul.114
  419.7 0.0 copy-done.2
  419.7 2.5 multiply_reduce_fusion.1
  422.2 0.0 copy-done.1
  422.2 1.6 fusion.18
  423.8 0.0 reduce-scatter.2.cloned.1.call-update
  425.1 141.1 %reduce-scatter.2.cloned.1.call-done = f32[32,128]{1,0:T(8,128)} async-done(((f32[2048,128]{1,0:T(8,128)}), f32[32,128]{1,0:T(8,128)}) %reduce-scatter.2.cloned.1.call-update) | async-done | bytes 16400 | tf_op jit(solution)/shard_map/reduce_scatter | solution.py:126
  566.2 31.5 %psum.22 = f32[32,128]{1,0:T(8,128)} all-reduce(f32[32,128]{1,0:T(8,128)} %reduce-scatter.2.cloned.1.call-done), channel_id=1, replica_groups=mesh['exp'=64,'rep'=8] {'rep'}, use_global_device_ids=true, to_apply=%region_12.13 | all-reduce | flops 4096 | bytes 32768 | tf_op jit(solution)/shard_map/psum | solution.py:134
  (14 shorter events, 0.2 us)
Async XLA Ops:
  7.2 310.3 %copy-start = (bf16[2048,128]{1,0:T(8,128)(2,1)S(1)}, bf16[2048,128]{1,0:T(8,128)(2,1)}, u32[]{:S(2)}) copy-start(bf16[2048,128]{1,0:T(8,128)(2,1)} %param.15) | copy-start | bytes 1572868
  7.2 124.3 %all-gather.5.cloned.1.call-start = ((), (), s32[]{:S(2)}) async-start(), calls=%async_computation.3 | async-start | bytes 3244032 | tf_op jit(solution)/shard_map/all_gather | solution.py:82
  7.9 129.2 %all-gather.7.cloned.1.call-start = ((), (), s32[]{:S(2)}) async-start(), calls=%async_computation.4 | async-start | bytes 3244032 | tf_op jit(solution)/shard_map/all_gather | solution.py:83
  23.0 105.1 %all-to-all-start = ((bf16[64,11,2048]{2,1,0:T(8,128)(2,1)}), bf16[64,11,2048]{2,1,0:T(8,128)(2,1)}, u32[]{:S(2)}, u32[]{:S(2)}) async-start(bf16[64,11,2048]{2,1,0:T(8,128)(2,1)} %reshape.185), calls=%async_computation | async-start | bytes 8388608 | tf_op jit(solution)/shard_map/all_to_all | solution.py:70
  33.7 148.2 %all-gather.9.cloned.1.call-start = ((), (), s32[]{:S(2)}) async-start(), calls=%async_computation.5 | async-start | bytes 3244032 | tf_op jit(solution)/shard_map/all_gather | solution.py:87
  197.1 10.6 %copy-start.4 = (bf16[16,32,128]{2,1,0:T(8,128)(2,1)S(1)}, bf16[16,32,128]{2,1,0:T(8,128)(2,1)}, u32[]{:S(2)}) copy-start(bf16[16,32,128]{2,1,0:T(8,128)(2,1)} %param.16) | copy-start | bytes 393220
  197.1 11.9 %copy-start.5 = (f32[180,2]{0,1:T(2,128)S(1)}, f32[180,2]{0,1:T(2,128)}, u32[]{:S(2)}) copy-start(f32[180,2]{0,1:T(2,128)} %param.11) | copy-start | bytes 4324
  197.1 104.8 %all-to-all-start.1 = ((bf16[64,11,2048]{2,1,0:T(8,128)(2,1)}), bf16[64,11,2048]{2,1,0:T(8,128)(2,1)}, u32[]{:S(2)}, u32[]{:S(2)}) async-start(bf16[64,11,2048]{2,1,0:T(8,128)(2,1)} %reshape.187), calls=%async_computation.1 | async-start | bytes 8388608 | tf_op jit(solution)/shard_map/all_to_all | solution.py:90
  207.6 110.4 %all-gather.11.cloned.1.call-start = ((), (), s32[]{:S(2)}) async-start(), calls=%async_computation.6 | async-start | bytes 1179648 | tf_op jit(solution)/shard_map/all_gather | solution.py:111
  208.7 357.5 %reduce-scatter.2.cloned.1.call-start = ((), (), s32[]{:S(2)}) async-start(), calls=%async_computation.7 | async-start | bytes 1064960 | tf_op jit(solution)/shard_map/reduce_scatter | solution.py:126
  311.7 5.6 copy-start.3
  317.5 104.7 %copy-start.1 = (bf16[180,2048]{1,0:T(8,128)(2,1)}, bf16[180,2048]{1,0:T(8,128)(2,1)S(1)}, u32[]{:S(2)}) copy-start(bf16[180,2048]{1,0:T(8,128)(2,1)S(1)} %add_convert_fusion) | copy-start | bytes 2211844
  317.5 4.5 copy-start.6
  318.0 101.6 %copy-start.2 = (bf16[128,32,128]{2,1,0:T(8,128)(2,1)S(1)}, bf16[128,32,128]{2,1,0:T(8,128)(2,1)}, u32[]{:S(2)}) copy-start(bf16[128,32,128]{2,1,0:T(8,128)(2,1)} %all-gather.11.cloned.1.call-done) | copy-start | bytes 3145732
Sparse Core Ops, SparseCore 0:
  10.0 59.7 all-gather.4
  71.8 53.6 all-gather.6
  127.5 54.4 all-gather.8
  210.2 40.1 all-gather.10
  423.9 142.2 reduce-scatter.1
where the time goes:
time: 606 us; the launch traced here: 605 us
  waiting for transfers between devices  374 us (62%)
  blocking collectives  128 us (21%)
  local copies, waits for them, and re-layouts  31.4 us (5%)
  matrix products  24.3 us (4%)
  starting transfers between devices  21.9 us (4%)
  between operations  16.5 us (3%)
  other arithmetic  9.89 us (2%)
    reduce_scatter x1, waiting for transfers between devices, body(): lax.psum_scatter(lax.dot_general(states, grad_vec, (((0,), (0,)), ((), ()...  141 us
    psum x1, blocking collectives, body(): lax.psum((jnp.sum(exp_logits, axis=0), jnp.sum(jnp.where(positive_hit, lo...  96.3 us
    all_to_all x1, waiting for transfers between devices, body(): lax.all_to_all(outgoing.reshape(experts, capacity, model_width), 'exp', s...  93.6 us
    all_to_all x1, waiting for transfers between devices, body(): lax.all_to_all(expert_out.reshape(experts, capacity, model_width), 'exp',...  92.1 us
    all_gather x1, waiting for transfers between devices, body(): lax.all_gather(down_weight, 'rep', axis=2, tiled=True)[0]  44.8 us
    psum x1, blocking collectives, body(): grad_projection = lax.psum(row_sums, 'rep')  31.5 us
  transfers between devices with their start and end apart: 7, of which 4 were waited for; matrix products, arithmetic and copies ran while one was open for 7% of the time, Pallas kernels for 0%

commit v1 on v0

--- a/solution.py
+++ b/solution.py
@@ -115,7 +115,10 @@
     positive_hit = owners[:, None] == positives[None, :]
     exp_logits = jnp.exp(logits)
     partition, pos_sum = lax.psum(
-        (jnp.sum(exp_logits, axis=0), jnp.sum(jnp.where(positive_hit, logits, 0.0))), ("exp", "rep")
+        lax.psum(
+            (jnp.sum(exp_logits, axis=0), jnp.sum(jnp.where(positive_hit, logits, 0.0))), "rep"
+        ),
+        "exp",
     )
     mean_loss = (jnp.sum(jnp.log(partition)) - pos_sum) / total_queries
     factor = exp_logits / partition[None, :] - positive_hit.astype(jnp.float32)

time: 606 us -> 649 us (1.071)
  blocking collectives: 128 us -> 165 us
    psum x0 -> x1, blocking collectives: none -> 116 us  [body(): lax.psum(lax.psum((jnp.sum(exp_logits, axis=0), jnp.sum(jnp.where(positiv...]
    psum x1, blocking collectives: 96.3 us -> 17.6 us  [body(): lax.psum((jnp.sum(exp_logits, axis=0), jnp.sum(jnp.where(positive_hit, lo...]
  transfers between devices with their start and end apart: 7 -> 7, of which waited for: 4 -> 4; matrix products, arithmetic and copies ran while one was open for 7% -> 6% of each run, Pallas kernels for 0% -> 0%
where the time goes in v1:
time: 649 us; the launch traced here: 648 us
  waiting for transfers between devices  379 us (58%)
  blocking collectives  165 us (25%)
  local copies, waits for them, and re-layouts  31.4 us (5%)
  matrix products  24.3 us (4%)
  starting transfers between devices  21.9 us (3%)
  between operations  16.5 us (3%)
  other arithmetic  9.89 us (2%)
    reduce_scatter x1, waiting for transfers between devices, body(): lax.psum_scatter(lax.dot_general(states, grad_vec, (((0,), (0,)), ((), ()...  146 us
    psum x1, blocking collectives, body(): lax.psum(lax.psum((jnp.sum(exp_logits, axis=0), jnp.sum(jnp.where(positiv...  116 us
    all_to_all x1, waiting for transfers between devices, body(): lax.all_to_all(outgoing.reshape(experts, capacity, model_width), 'exp', s...  93.6 us
    all_to_all x1, waiting for transfers between devices, body(): lax.all_to_all(expert_out.reshape(experts, capacity, model_width), 'exp',...  92.1 us
    all_gather x1, waiting for transfers between devices, body(): lax.all_gather(down_weight, 'rep', axis=2, tiled=True)[0]  44.8 us
    psum x1, blocking collectives, body(): grad_projection = lax.psum(row_sums, 'rep')  31.4 us
    psum x1, blocking collectives, body(): lax.psum((jnp.sum(exp_logits, axis=0), jnp.sum(jnp.where(positive_hit, lo...  17.6 us
  transfers between devices with their start and end apart: 7, of which 4 were waited for; matrix products, arithmetic and copies ran while one was open for 6% of the time, Pallas kernels for 0%

profile of v1, /device:TPU:16, one launch (start us, length us, event | category | flops | bytes accessed | tf_op | source)
XLA Modules:
  0.0 648.1 jit_solution(5905416403461974906)
XLA Ops:
  7.2 0.0 copy-start
  7.2 0.0 all-gather.5.cloned.1.call-start
  7.2 0.7 all-gather.5.cloned.1.call-update
  7.9 0.0 all-gather.7.cloned.1.call-start
  8.0 0.7 all-gather.7.cloned.1.call-update
  8.7 0.8 copy.20
  9.5 0.1 eq.31
  9.7 0.9 reduce-window.6
  10.6 0.2 slice_reduce_fusion
  10.8 0.7 broadcast_multiply_fusion
  11.5 0.1 copy.19
  11.6 0.1 mul.100
  11.8 0.1 bitcast_bitcast_fusion
  12.0 8.1 %scatter_custom_fusion = bf16[704,2048]{1,0:T(8,128)(2,1)S(1)} fusion(s32[360]{0:T(512)S(1)} %fusion.22, bf16[180,2048]{1,0:T(8,128)(2,1)} %param.9, s32[1024]{0:T(1024)S(1)} %pad_clamp_fusion.1, bf16[]{:T(256)} %constant.21.clone.1), kind=kCustom, calls=%fused_computation.16 | custom fusion | bytes 2884096 | tf_op jit(solution)/shard_map/scatter | solution.py:68
  20.1 2.9 reshape.185
  23.0 10.8 %all-to-all-start = ((bf16[64,11,2048]{2,1,0:T(8,128)(2,1)}), bf16[64,11,2048]{2,1,0:T(8,128)(2,1)}, u32[]{:S(2)}, u32[]{:S(2)}) async-start(bf16[64,11,2048]{2,1,0:T(8,128)(2,1)} %reshape.185), calls=%async_computation | async-start | bytes 8388608 | tf_op jit(solution)/shard_map/all_to_all | solution.py:70
  33.7 0.2 all-gather.9.cloned.1.call-start
  34.0 0.5 all-gather.9.cloned.1.call-update
  34.5 93.6 %all-to-all-done = bf16[64,11,2048]{2,1,0:T(8,128)(2,1)} async-done(((bf16[64,11,2048]{2,1,0:T(8,128)(2,1)}), bf16[64,11,2048]{2,1,0:T(8,128)(2,1)}, u32[]{:S(2)}, u32[]{:S(2)}) %all-to-all-start) | async-done | bytes 2883616 | tf_op jit(solution)/shard_map/all_to_all | solution.py:70
  128.1 3.4 reshape.186
  131.5 0.0 all-gather.5.cloned.1.call-done
  131.5 5.6 fusion.4
  137.1 44.8 %all-gather.9.cloned.1.call-done = bf16[1,704,2048]{2,1,0:T(8,128)(2,1)} async-done(((bf16[1,704,256]{2,1,0:T(8,128)(2,1)}), bf16[1,704,2048]{2,1,0:T(8,128)(2,1)}) %all-gather.9.cloned.1.call-update) | async-done | bytes 2883600 | tf_op jit(solution)/shard_map/all_gather | solution.py:87
  181.9 10.4 %convolution_convert_fusion = bf16[704,2048]{1,0:T(8,128)(2,1)} fusion(bf16[1,704,2048]{2,1,0:T(8,128)(2,1)} %all-gather.9.cloned.1.call-done, f32[704,704]{1,0:T(8,128)} %fusion.4, bf16[704,2048]{1,0:T(8,128)(2,1)S(1)} %reshape.186, bf16[1,2048,704]{1,2,0:T(8,128)(2,1)} %all-gather.7.cloned.1.call-done), kind=kOutput, calls=%fused_computation.5 | convolution fusion | flops 4064501760 | bytes 13516800 | tf_op jit(solution)/shard_map/dot_general | solution.py:85
  192.3 4.8 reshape.187
  197.1 10.5 %all-to-all-start.1 = ((bf16[64,11,2048]{2,1,0:T(8,128)(2,1)}), bf16[64,11,2048]{2,1,0:T(8,128)(2,1)}, u32[]{:S(2)}, u32[]{:S(2)}) async-start(bf16[64,11,2048]{2,1,0:T(8,128)(2,1)} %reshape.187), calls=%async_computation.1 | async-start | bytes 8388608 | tf_op jit(solution)/shard_map/all_to_all | solution.py:90
  207.6 0.0 all-gather.11.cloned.1.call-start
  207.7 0.0 copy-done.4
  207.7 0.1 fusion.14
  207.8 0.8 fusion.15
  208.6 0.0 all-gather.11.cloned.1.call-update
  208.7 0.3 reduce-scatter.2.cloned.1.call-start
  208.9 0.0 copy-done.5
  209.0 0.8 copy.18
  209.7 92.1 %all-to-all-done.1 = bf16[64,11,2048]{2,1,0:T(8,128)(2,1)} async-done(((bf16[64,11,2048]{2,1,0:T(8,128)(2,1)}), bf16[64,11,2048]{2,1,0:T(8,128)(2,1)}, u32[]{:S(2)}, u32[]{:S(2)}) %all-to-all-start.1) | async-done | bytes 2883616 | tf_op jit(solution)/shard_map/all_to_all | solution.py:90
  301.9 3.4 reshape.188
  305.3 3.1 gather_fusion
  308.4 3.4 reshape.191
  311.7 0.0 copy-start.3
  311.8 5.6 multiply_reduce_fusion
  317.3 0.0 copy-done.3
  317.3 0.2 add_convert_fusion
  317.5 0.0 copy-done
  317.5 0.0 copy-start.1
  317.5 0.0 copy-start.6
  317.5 0.5 multiply_reduce_fusion.2
  318.0 0.0 all-gather.11.cloned.1.call-done
  318.0 0.0 copy-start.2
  318.0 3.8 fusion.28
  321.9 0.1 mul.109
  321.9 0.1 reduce_sum.93
  322.0 0.0 copy-done.6
  322.1 0.6 fusion.26
  322.7 17.6 %all-reduce.2 = (f32[128]{0:T(128)S(1)}, f32[]{:T(128)}) all-reduce(f32[128]{0:T(128)S(1)} %get-tuple-element.10, f32[]{:T(128)} %get-tuple-element.9), channel_id=1, replica_groups=mesh['exp'=64,'rep'=8] {'rep'}, use_global_device_ids=true, to_apply=%region_9.10 | all-reduce | flops 129 | bytes 1032 | tf_op jit(solution)/shard_map/psum | solution.py:118
  340.3 116.0 %all-reduce.1 = (f32[128]{0:T(128)S(1)}, f32[]{:T(128)}) all-reduce(f32[128]{0:T(128)S(1)} %get-tuple-element.5, f32[]{:T(128)} %get-tuple-element.6), channel_id=1, replica_groups=mesh['exp'=64,'rep'=8] {'exp'}, use_global_device_ids=true, to_apply=%region_10.11 | all-reduce | flops 129 | bytes 1032 | tf_op jit(solution)/shard_map/psum | solution.py:117
  456.3 0.6 log_reduce_fusion
  456.9 0.1 mul.113
  457.0 0.1 mul.114
  457.1 0.0 copy-done.2
  457.1 2.5 multiply_reduce_fusion.1
  459.6 1.6 fusion.18
  461.2 0.0 reduce-scatter.2.cloned.1.call-update
  462.5 146.5 %reduce-scatter.2.cloned.1.call-done = f32[32,128]{1,0:T(8,128)} async-done(((f32[2048,128]{1,0:T(8,128)}), f32[32,128]{1,0:T(8,128)}) %reduce-scatter.2.cloned.1.call-update) | async-done | bytes 16400 | tf_op jit(solution)/shard_map/reduce_scatter | solution.py:129
  609.0 31.4 %psum.37 = f32[32,128]{1,0:T(8,128)} all-reduce(f32[32,128]{1,0:T(8,128)} %reduce-scatter.2.cloned.1.call-done), channel_id=1, replica_groups=mesh['exp'=64,'rep'=8] {'rep'}, use_global_device_ids=true, to_apply=%region_13.14 | all-reduce | flops 4096 | bytes 32768 | tf_op jit(solution)/shard_map/psum | solution.py:137
  (15 shorter events, 0.2 us)
Async XLA Ops:
  7.2 310.3 %copy-start = (bf16[2048,128]{1,0:T(8,128)(2,1)S(1)}, bf16[2048,128]{1,0:T(8,128)(2,1)}, u32[]{:S(2)}) copy-start(bf16[2048,128]{1,0:T(8,128)(2,1)} %param.15) | copy-start | bytes 1572868
  7.2 124.3 %all-gather.5.cloned.1.call-start = ((), (), s32[]{:S(2)}) async-start(), calls=%async_computation.3 | async-start | bytes 3244032 | tf_op jit(solution)/shard_map/all_gather | solution.py:82
  7.9 129.2 %all-gather.7.cloned.1.call-start = ((), (), s32[]{:S(2)}) async-start(), calls=%async_computation.4 | async-start | bytes 3244032 | tf_op jit(solution)/shard_map/all_gather | solution.py:83
  23.0 105.1 %all-to-all-start = ((bf16[64,11,2048]{2,1,0:T(8,128)(2,1)}), bf16[64,11,2048]{2,1,0:T(8,128)(2,1)}, u32[]{:S(2)}, u32[]{:S(2)}) async-start(bf16[64,11,2048]{2,1,0:T(8,128)(2,1)} %reshape.185), calls=%async_computation | async-start | bytes 8388608 | tf_op jit(solution)/shard_map/all_to_all | solution.py:70
  33.7 148.2 %all-gather.9.cloned.1.call-start = ((), (), s32[]{:S(2)}) async-start(), calls=%async_computation.5 | async-start | bytes 3244032 | tf_op jit(solution)/shard_map/all_gather | solution.py:87
  197.1 10.6 %copy-start.4 = (bf16[16,32,128]{2,1,0:T(8,128)(2,1)S(1)}, bf16[16,32,128]{2,1,0:T(8,128)(2,1)}, u32[]{:S(2)}) copy-start(bf16[16,32,128]{2,1,0:T(8,128)(2,1)} %param.16) | copy-start | bytes 393220
  197.1 11.9 %copy-start.5 = (f32[180,2]{0,1:T(2,128)S(1)}, f32[180,2]{0,1:T(2,128)}, u32[]{:S(2)}) copy-start(f32[180,2]{0,1:T(2,128)} %param.11) | copy-start | bytes 4324
  197.1 104.8 %all-to-all-start.1 = ((bf16[64,11,2048]{2,1,0:T(8,128)(2,1)}), bf16[64,11,2048]{2,1,0:T(8,128)(2,1)}, u32[]{:S(2)}, u32[]{:S(2)}) async-start(bf16[64,11,2048]{2,1,0:T(8,128)(2,1)} %reshape.187), calls=%async_computation.1 | async-start | bytes 8388608 | tf_op jit(solution)/shard_map/all_to_all | solution.py:90
  207.6 110.4 %all-gather.11.cloned.1.call-start = ((), (), s32[]{:S(2)}) async-start(), calls=%async_computation.6 | async-start | bytes 1179648 | tf_op jit(solution)/shard_map/all_gather | solution.py:111
  208.7 400.4 %reduce-scatter.2.cloned.1.call-start = ((), (), s32[]{:S(2)}) async-start(), calls=%async_computation.7 | async-start | bytes 1064960 | tf_op jit(solution)/shard_map/reduce_scatter | solution.py:129
  311.7 5.6 copy-start.3
  317.5 142.1 %copy-start.1 = (bf16[180,2048]{1,0:T(8,128)(2,1)}, bf16[180,2048]{1,0:T(8,128)(2,1)S(1)}, u32[]{:S(2)}) copy-start(bf16[180,2048]{1,0:T(8,128)(2,1)S(1)} %add_convert_fusion) | copy-start | bytes 2211844
  317.5 4.5 copy-start.6
  318.0 139.1 %copy-start.2 = (bf16[128,32,128]{2,1,0:T(8,128)(2,1)S(1)}, bf16[128,32,128]{2,1,0:T(8,128)(2,1)}, u32[]{:S(2)}) copy-start(bf16[128,32,128]{2,1,0:T(8,128)(2,1)} %all-gather.11.cloned.1.call-done) | copy-start | bytes 3145732
Sparse Core Ops, SparseCore 0:
  10.0 59.7 all-gather.4
  71.8 53.6 all-gather.6
  127.5 54.4 all-gather.8
  210.2 40.1 all-gather.10
  461.3 147.6 reduce-scatter.1
